TPU v7x, 768 devices: a whole 4x8x12 slice. The times are simulated.
768 devices in a mesh: dp: 64 (over z_hi, y, x), tensor: 12 (over z_lo, core).
Axes of the slice: x: 4, y: 8, z: 12 (z_hi: 2, z_lo: 6; z = z_hi * 6 + z_lo), core: 2. Of those that a mesh axis runs over, the one named last changes fastest.
Arguments:
- mantissas: bfloat16 [12288, 3072], P(('dp', 'tensor')), may hold values from -24 to 24
- exponents: int32 [12288, 24], P(('dp', 'tensor')), may hold values from -3 to 1
- weight: bfloat16 [3072, 7680], P(None, 'tensor'), may hold values from -0.109375 to 0.109375
- cotangent: bfloat16 [12288, 7680], P('dp', 'tensor'), may hold values from -16 to 16
Outputs:
- output: bfloat16 [12288, 7680], P('dp', 'tensor')
- grad_input: bfloat16 [12288, 3072], P(('dp', 'tensor'))
- grad_weight: float32 [3072, 7680], P('dp', 'tensor')
Inputs may be any that keep to these rules, and one draw needn't show every extreme that they name: `exponents`: base-two exponent of a block of 128 features.
All inputs are finite; a program needn't handle non-finite values.
Results may differ from a plain program's by a relative error of at most 0.02.
Values may be sent and summed in bfloat16 or wider, within the bound.
A program may use at most 64 MiB of HBM per device.

v0:
```python
import math

import jax
import jax.numpy as jnp
from jax import lax
from jax.sharding import PartitionSpec as P


def dequantize(mantissas, exponents):
    factors = jnp.exp2(exponents.astype(jnp.float32))
    token_count = mantissas.shape[0]
    blocks = (
        mantissas.astype(jnp.float32).reshape(token_count, exponents.shape[1], 128)
        * factors[:, :, None]
    )
    return blocks.reshape(token_count, mantissas.shape[1]).astype(jnp.bfloat16)


def body(mantissas, exponents, weight, cotangent):
    local_rows = dequantize(mantissas, exponents)
    gathered = lax.all_gather(local_rows, "tensor", axis=0, tiled=True)
    linear = jnp.dot(gathered, weight, preferred_element_type=jnp.float32)
    output = jax.nn.silu(linear).astype(jnp.bfloat16)
    sigmoid = jax.nn.sigmoid(linear)
    grad_linear = (
        cotangent.astype(jnp.float32) * sigmoid * (1.0 + linear * (1.0 - sigmoid))
    ).astype(jnp.bfloat16)
    grad_input = lax.psum_scatter(
        lax.dot_general(
            grad_linear, weight, (((1,), (1,)), ((), ())), preferred_element_type=jnp.float32
        ).astype(jnp.bfloat16),
        "tensor",
        scatter_dimension=0,
        tiled=True,
    )
    factor = 1.0 / math.sqrt(lax.axis_size("dp") * gathered.shape[0])
    summed = lax.psum_scatter(
        lax.dot_general(
            gathered, grad_linear, (((0,), (0,)), ((), ())), preferred_element_type=jnp.float32
        ),
        "dp",
        scatter_dimension=0,
        tiled=True,
    )
    grad_weight = summed * factor
    return (output, grad_input, grad_weight)


def solution(mesh):
    return jax.shard_map(
        body,
        mesh=mesh,
        in_specs=(
            P(("dp", "tensor"), None),
            P(("dp", "tensor"), None),
            P(None, "tensor"),
            P("dp", "tensor"),
        ),
        out_specs=(P("dp", "tensor"), P(("dp", "tensor"), None), P("dp", "tensor")),
        check_vma=False,
    )
```

profile of v0, /device:TPU:6, one launch (start us, length us, event | category | flops | bytes accessed | tf_op | source)
XLA Modules:
  0.0 1082.8 jit_solution(7017047746503721958)
XLA Ops:
  7.2 0.0 all-gather.2.cloned.1.call-start
  7.2 0.7 multiply_exponential_fusion
  7.9 0.1 mul.30
  8.0 1.6 fusion
  9.6 0.0 all-gather.2.cloned.1.call-update
  9.6 0.0 copy-start.1
  9.6 0.0 reduce-scatter.5.cloned.1.call-start
  9.7 75.7 %all-gather.2.cloned.1.call-done = bf16[192,3072]{1,0:T(8,128)(2,1)} async-done(((bf16[16,3072]{1,0:T(8,128)(2,1)}), bf16[192,3072]{1,0:T(8,128)(2,1)}) %all-gather.2.cloned.1.call-update) | async-done | bytes 1179664 | tf_op jit(solution)/shard_map/all_gather | solution.py:21
  85.4 0.0 copy-start
  85.4 4.4 multiply_convert_fusion.1
  89.7 0.0 copy-done.1
  89.7 0.0 copy-done
  89.7 4.6 fusion.1
  94.3 0.0 reduce-scatter.5.cloned.1.call-update
  94.3 0.0 reduce-scatter.3.cloned.1.call-start
  94.4 4.7 convolution_convert_fusion
  99.1 0.0 reduce-scatter.3.cloned.1.call-update
  99.1 906.8 %reduce-scatter.5.cloned.1.call-done = f32[48,640]{1,0:T(8,128)} async-done(((f32[3072,640]{1,0:T(8,128)}), f32[48,640]{1,0:T(8,128)}) %reduce-scatter.5.cloned.1.call-update) | async-done | bytes 122896 | tf_op jit(solution)/shard_map/reduce_scatter | solution.py:37
  1005.9 1.6 broadcast_multiply_fusion
  1007.4 68.9 %reduce-scatter.3.cloned.1.call-done = bf16[16,3072]{1,0:T(8,128)(2,1)} async-done(((bf16[192,3072]{1,0:T(8,128)(2,1)}), bf16[16,3072]{1,0:T(8,128)(2,1)}) %reduce-scatter.3.cloned.1.call-update) | async-done | bytes 98320 | tf_op jit(solution)/shard_map/reduce_scatter | solution.py:28
Async XLA Ops:
  7.2 78.2 %all-gather.2.cloned.1.call-start = ((), (), s32[]{:S(2)}) async-start(), calls=%async_computation.2 | async-start | bytes 1277952 | tf_op jit(solution)/shard_map/all_gather | solution.py:21
  9.6 80.1 %copy-start.1 = (bf16[192,640]{1,0:T(8,128)(2,1)S(1)}, bf16[192,640]{1,0:T(8,128)(2,1)}, u32[]{:S(2)}) copy-start(bf16[192,640]{1,0:T(8,128)(2,1)} %param.7) | copy-start | bytes 737284
  9.6 996.2 %reduce-scatter.5.cloned.1.call-start = ((), (), s32[]{:S(2)}) async-start(), calls=%async_computation.4 | async-start | bytes 7987200 | tf_op jit(solution)/shard_map/reduce_scatter | solution.py:37
  85.4 4.4 copy-start
  94.3 982.0 %reduce-scatter.3.cloned.1.call-start = ((), (), s32[]{:S(2)}) async-start(), calls=%async_computation.3 | async-start | bytes 1277952 | tf_op jit(solution)/shard_map/reduce_scatter | solution.py:28
Sparse Core Ops, SparseCore 0:
  11.0 74.3 all-gather.1
  94.5 911.3 reduce-scatter.4
  1009.9 66.3 reduce-scatter.2
where the time goes:
time: 1080 us
  waiting for transfers between devices  1050 us (97%)
  between operations  13.8 us (1%)
  matrix products  13.6 us (1%)
    reduce_scatter x1, waiting for transfers between devices, body(): lax.psum_scatter(lax.dot_general(gathered, grad_linear, (((0,), (0,)), ((...  907 us
    all_gather x1, waiting for transfers between devices, body(): gathered = lax.all_gather(local_rows, 'tensor', axis=0, tiled=True)  75.7 us
    reduce_scatter x1, waiting for transfers between devices, body(): lax.psum_scatter(lax.dot_general(grad_linear, weight, (((1,), (1,)), ((),...  68.9 us
  transfers between devices with their start and end apart: 3, of which 3 were waited for; matrix products, arithmetic and copies ran while one was open for 1% of the time, Pallas kernels for 0%

commit v1 on v0

v1 whole, which is shorter than its diff:
```python
import functools
import math
from types import SimpleNamespace

import jax
import jax.numpy as jnp
from jax import lax
from jax.experimental import pallas as pl
from jax.experimental.pallas import tpu as pltpu
from jax.sharding import PartitionSpec as P

MESH = pl.DeviceIdType.MESH
F32, BF16 = jnp.float32, jnp.bfloat16

SIZES = SimpleNamespace(H=2, Y=8, X=4, Z=6, C=2, B=16, R=48, F=640)


def permute_tiles(tiles, size, out_chunk_source):
    lane = lax.broadcasted_iota(jnp.int32, tiles[0].shape, 1)
    result = []
    for k in range(len(tiles)):
        runs = []
        for l in range(128):
            o = k * 128 + l
            src = out_chunk_source(o // size) * size + o % size
            key = (src // 128, (l - src) % 128)
            if runs and runs[-1][0] == key:
                runs[-1][2] = l + 1
            else:
                runs.append([key, l, l + 1])
        out = None
        for (tile, shift), lo, hi in runs:
            piece = tiles[tile]
            if shift:
                piece = pltpu.roll(piece, shift, 1)
            out = piece if out is None else jnp.where(lane >= lo, piece, out)
        result.append(out)
    return result


def kernel(
    n,
    mant, expo, w_hbm, ct_hbm,
    out_hbm, dx_out, dw_out,
    wp, wn, ct, xg, lin, xq, gq, outv, prt, psib, rr, rl, sr, sl, acc, ysend, yrecv, tu, hsend, hrecv,
    loc, ag_s, ag_r, sib_s, sib_r, xs_s, xs_r, xb_s, xb_r, g_s, g_r, p_s, p_r, dx_s, dx_r, y_s, y_r, h_s, h_r,
):
    H, Y, X, Z, C, B, R, F = n.H, n.Y, n.X, n.Z, n.C, n.B, n.R, n.F
    HY = H * Y
    D = HY * X * R
    Q = D // X
    TH = Z * B
    T = C * TH
    S = n.S
    SB = D // S
    YH = Y // 2

    dp = lax.axis_index("dp")
    tp = lax.axis_index("tensor")
    x = lax.rem(dp, X)
    y = lax.rem(dp // X, Y)
    h = dp // (X * Y)
    c = lax.rem(tp, C)
    z = tp // C
    plane = dp - x

    sib = (dp, tp + 1 - 2 * c)
    z_right = (dp, tp + C)
    z_left = (dp, tp - C)
    x_by = {k: (plane + lax.rem(x + k, X), tp) for k in (1, 2, 3)}
    y_by = [
        ((h * Y + lax.rem(y + 1, Y)) * X + x, tp),
        ((h * Y + lax.rem(y + Y - 1, Y)) * X + x, tp),
    ]
    h_by = (((1 - h) * Y + y) * X + x, tp)

    def remote(src, dst, send, recv, device):
        return pltpu.make_async_remote_copy(
            src_ref=src, dst_ref=dst, send_sem=send, recv_sem=recv,
            device_id=device, device_id_type=MESH,
        )

    def arrived(dst, recv):
        remote(dst, dst, recv, recv, sib).wait_recv()

    def sent(src, send):
        remote(src, src, send, send, sib).wait_send()

    barrier = pltpu.get_barrier_semaphore()
    ring = [
        (dp, lax.rem(tp + C, Z * C)),
        (dp, lax.rem(tp + Z * C - C, Z * C)),
    ]
    greeted = [sib, *ring, x_by[1], x_by[2], x_by[3], *y_by, h_by]
    for device in greeted:
        pl.semaphore_signal(barrier, inc=1, device_id=device, device_id_type=MESH)

    w_in = [pltpu.make_async_copy(w_hbm.at[:, k], wp.at[k], loc.at[k]) for k in range(X)]
    ct_in = [pltpu.make_async_copy(ct_hbm.at[:, k], ct.at[k], loc.at[X + k]) for k in range(C)]
    wn_in = pltpu.make_async_copy(w_hbm, wn, loc.at[X + C])
    for copy in [*w_in, *ct_in, wn_in]:
        copy.start()

    def rows(core, q):
        return pl.ds(pl.multiple_of(core * TH + q * B, B), B)

    factors = jnp.exp2(expo[...].astype(F32))
    tiles = [
        mant[:, pl.ds(128 * b, 128)].astype(F32) * factors[:, b : b + 1]
        for b in range(D // 128)
    ]
    for k, tile in enumerate(permute_tiles(tiles, R, lambda j: (j % HY) * X + j // HY)):
        xg[rows(c, z), pl.ds(128 * k, 128)] = tile.astype(BF16)

    pl.semaphore_wait(barrier, len(greeted))

    def hop(way, step, sub, q):
        part = xg.at[rows(c, q), pl.ds(sub * SB, SB)]
        return remote(
            part, part, ag_s.at[way, step, sub], ag_r.at[way, step, sub],
            z_right if way == 0 else z_left,
        )

    def spread_sibling(q):
        part = xg.at[rows(c, q), :]
        return remote(part, part, sib_s.at[q], sib_r.at[q], sib)

    def spread_x(q, k):
        to = lax.rem(x + k, X)
        return remote(
            xg.at[rows(c, q), pl.ds(pl.multiple_of(to * Q, Q), Q)],
            xq.at[k - 1, rows(c, q), :],
            xs_s.at[k - 1], xs_r.at[k - 1], x_by[k],
        )

    def spread(q):
        spread_sibling(q).start()
        for k in (1, 3, 2):
            spread_x(q, k).start()

    for sub in range(S):
        @pl.when(z < Z - 1)
        def _():
            hop(0, 0, sub, z).start()

        @pl.when(z > 0)
        def _():
            hop(1, 0, sub, z).start()

    spread(z)
    for s in range(Z - 1):
        from_left = z - 1 - s
        from_right = z + 1 + s
        for sub in range(S):
            @pl.when(from_left >= 0)
            def _():
                hop(0, s, sub, from_left).wait_recv()
                if s + 1 < Z - 1:
                    @pl.when(z < Z - 1)
                    def _():
                        hop(0, s + 1, sub, from_left).start()

            @pl.when(from_right <= Z - 1)
            def _():
                hop(1, s, sub, from_right).wait_recv()
                if s + 1 < Z - 1:
                    @pl.when(z > 0)
                    def _():
                        hop(1, s + 1, sub, from_right).start()

        @pl.when(from_left >= 0)
        def _():
            spread(from_left)

        @pl.when(from_right <= Z - 1)
        def _():
            spread(from_right)

    for q in range(Z):
        arrived(xg.at[rows(1 - c, q), :], sib_r.at[q])

    for k in range(X):
        w_in[k].wait()
        part = jnp.dot(
            xg[:, pl.ds(k * Q, Q)], wp[k].reshape(Q, F), preferred_element_type=F32
        )
        if k == 0:
            lin[...] = part
        else:
            lin[...] += part
    for copy in ct_in:
        copy.wait()
    linear = lin[...]
    sigmoid = jax.nn.sigmoid(linear)
    cot = ct[...].reshape(T, F).astype(F32)
    gq[0] = (cot * sigmoid * (1.0 + linear * (1.0 - sigmoid))).astype(BF16)

    def g_part(i):
        slot, half, k = [(1, 0, 1), (3, 1, 3), (1, 1, 1), (3, 0, 3)][i]
        where = pl.ds(half * TH, TH)
        return remote(gq.at[0, where], gq.at[slot, where], g_s.at[i], g_r.at[i], x_by[k])

    def g_forward(i):
        where = pl.ds(i * TH, TH)
        return remote(
            gq.at[1 if i == 0 else 3, where], gq.at[2, where], g_s.at[4 + i], g_r.at[4 + i],
            x_by[1 if i == 0 else 3],
        )

    for i in range(4):
        g_part(i).start()

    outv[...] = (linear * sigmoid).astype(BF16).reshape(C, Z, B, F)
    out_back = [
        pltpu.make_async_copy(outv.at[k], out_hbm.at[:, k], loc.at[X + C + 1 + k]) for k in range(C)
    ]
    for copy in out_back:
        copy.start()

    def x_sibling(k):
        part = xq.at[k - 1, pl.ds(pl.multiple_of(c * TH, TH), TH), :]
        return remote(part, part, xb_s.at[k - 1], xb_r.at[k - 1], sib)

    for k in (1, 3, 2):
        arrived(xq.at[k - 1, pl.ds(0, TH), :], xs_r.at[k - 1])
        x_sibling(k).start()

    wn_in.wait()
    NC = X
    ND = D // NC

    def p_sibling(k):
        columns = pl.ds(k * ND, ND)
        return remote(
            prt.at[pl.ds(pl.multiple_of((1 - c) * TH, TH), TH), columns], psib.at[:, columns],
            p_s.at[k], p_r.at[k], sib,
        )

    for k in range(NC):
        part = lax.dot_general(
            gq[0], wn[pl.ds(k * (HY // NC), HY // NC)].reshape(ND, F),
            (((1,), (1,)), ((), ())), preferred_element_type=F32,
        )
        prt[:, pl.ds(k * ND, ND)] = part.astype(BF16)
        p_sibling(k).start()

    for i in range(2):
        g_part(i).wait_recv()
        g_forward(i).start()

    for k in range(NC):
        p_sibling(k).wait_recv()

    def pair(q):
        own = prt[rows(c, q), :].astype(F32)
        return own + psib[pl.ds(pl.multiple_of(q * B, B), B), :].astype(F32)

    def dx_hop(way, j):
        return remote(
            (sr, sl)[way].at[j], (rr, rl)[way].at[j], dx_s.at[way, j], dx_r.at[way, j],
            (z_right, z_left)[way],
        )

    def dx_slot(t):
        for way, first in ((0, z), (1, Z - 1 - z)):
            j = t - first
            q = Z - 1 - j if way == 0 else j
            out, came = (sr, sl)[way], (rr, rl)[way]

            @pl.when(first == 0)
            def _():
                out[j] = pair(q).astype(BF16)
                dx_hop(way, j).start()

            if t > 0:
                @pl.when((first > 0) & (j >= 0))
                def _():
                    dx_hop(way, j).wait_recv()
                    out[j] = (pair(q) + came[j].astype(F32)).astype(BF16)
                    dx_hop(way, j).start()

    def dw_slot(k):
        if k == 0:
            left = xg[:, pl.ds(pl.multiple_of(x * Q, Q), Q)]
        else:
            left = xq[k - 1]
        part = lax.dot_general(
            left, gq[k], (((0,), (0,)), ((), ())), preferred_element_type=F32
        )
        if k == 0:
            acc[...] = part
        else:
            acc[...] += part

    dx_slot(0)
    dw_slot(0)
    for k in (1, 3, 2):
        x_sibling(k).wait_recv()
    g_part(2).wait_recv()
    dw_slot(1)
    if Z > 2:
        dx_slot(1)
    g_part(3).wait_recv()
    dw_slot(3)
    for i in range(2):
        g_forward(i).wait_recv()
    dw_slot(2)

    def y_hop(way, u, s):
        return remote(
            ysend.at[way, u, s - 1], yrecv.at[way, u, s - 1],
            y_s.at[way, u, s - 1], y_r.at[way, u, s - 1], y_by[way],
        )

    def y_rows(u, to):
        return pl.ds(pl.multiple_of((u * Y + to) * R, R), R)

    def first_step(way, u):
        return 1 if way == u else 2

    def y_step(s):
        for i in range(2):
            for way in range(2):
                u = way if i == 0 else 1 - way
                start = first_step(way, u)
                if s < start or s > YH:
                    continue
                away = YH + 1 - s
                to = lax.rem(y + (away if way == 0 else Y - away), Y)
                value = acc[y_rows(u, to), :]
                if s > start:
                    y_hop(way, u, s - 1).wait_recv()
                    value = value + yrecv[way, u, s - 2].astype(F32)
                ysend[way, u, s - 1] = value.astype(BF16)
                y_hop(way, u, s).start()

    slot = 2
    for s in range(1, YH + 1):
        y_step(s)
        if slot < Z - 1:
            dx_slot(slot)
            slot += 1
    while slot < Z - 1:
        dx_slot(slot)
        slot += 1

    for u in range(H):
        value = acc[y_rows(u, y), :]
        for way in range(2):
            if first_step(way, u) <= YH:
                y_hop(way, u, YH).wait_recv()
                value = value + yrecv[way, u, YH - 1].astype(F32)
        tu[u] = value
    hsend[...] = tu[1 - h].astype(BF16)
    across = remote(hsend, hrecv, h_s, h_r, h_by)
    across.start()

    lin_dx = pair(z)

    @pl.when(z == 0)
    def _():
        arrived(rl.at[0], dx_r.at[1, 0])
        dx_out[...] = (lin_dx + rl[0].astype(F32)).astype(BF16)

    @pl.when(z == Z - 1)
    def _():
        arrived(rr.at[0], dx_r.at[0, 0])
        dx_out[...] = (lin_dx + rr[0].astype(F32)).astype(BF16)

    @pl.when((z > 0) & (z < Z - 1))
    def _():
        arrived(rr.at[Z - 1 - z], dx_r.at[0, Z - 1 - z])
        arrived(rl.at[z], dx_r.at[1, z])
        dx_out[...] = (lin_dx + rr[Z - 1 - z].astype(F32) + rl[z].astype(F32)).astype(BF16)

    across.wait_recv()
    factor = 1.0 / math.sqrt(H * Y * X * T)
    dw_out[...] = (tu[h] + hrecv[...].astype(F32)) * factor

    for copy in out_back:
        copy.wait()
    for sub in range(S):
        for s in range(Z - 1):
            @pl.when((z - s >= 0) & (z < Z - 1))
            def _():
                hop(0, s, sub, z - s).wait_send()

            @pl.when((z + s <= Z - 1) & (z > 0))
            def _():
                hop(1, s, sub, z + s).wait_send()
    for q in range(Z):
        spread_sibling(q).wait_send()
    for k in (1, 2, 3):
        sent(xq.at[k - 1, pl.ds(0, TH), :], xs_s.at[k - 1])
        x_sibling(k).wait_send()
    for i in range(4):
        g_part(i).wait_send()
    for i in range(2):
        g_forward(i).wait_send()
    for k in range(NC):
        p_sibling(k).wait_send()
    for j in range(Z - 1):
        @pl.when(Z - 1 - j > z)
        def _():
            dx_hop(0, j).wait_send()

        @pl.when(j < z)
        def _():
            dx_hop(1, j).wait_send()
    for way in range(2):
        for u in range(2):
            for s in range(first_step(way, u), YH + 1):
                y_hop(way, u, s).wait_send()
    across.wait_send()


def body(n, mantissas, exponents, weight, cotangent):
    H, Y, X, Z, C, B, R, F = n.H, n.Y, n.X, n.Z, n.C, n.B, n.R, n.F
    HY = H * Y
    D = HY * X * R
    Q, TH, T, S, YH = D // X, Z * B, Z * B * C, n.S, Y // 2
    anywhere = pl.BlockSpec(memory_space=pl.ANY)
    vmem = pl.BlockSpec(memory_space=pltpu.VMEM)
    dma = pltpu.SemaphoreType.DMA
    out, dx, dw = pl.pallas_call(
        functools.partial(kernel, n),
        out_shape=(
            jax.ShapeDtypeStruct((Z, C, B, F), BF16),
            jax.ShapeDtypeStruct((B, D), BF16),
            jax.ShapeDtypeStruct((R, F), F32),
        ),
        in_specs=[vmem, vmem, anywhere, anywhere],
        out_specs=(anywhere, vmem, vmem),
        scratch_shapes=[
            pltpu.VMEM((X, HY, R, F), BF16),
            pltpu.VMEM((HY, X, R, F), BF16),
            pltpu.VMEM((C, Z, B, F), BF16),
            pltpu.VMEM((T, D), BF16),
            pltpu.VMEM((T, F), F32),
            pltpu.VMEM((3, T, Q), BF16),
            pltpu.VMEM((4, T, F), BF16),
            pltpu.VMEM((C, Z, B, F), BF16),
            pltpu.VMEM((T, D), BF16),
            pltpu.VMEM((TH, D), BF16),
            pltpu.VMEM((Z - 1, B, D), BF16),
            pltpu.VMEM((Z - 1, B, D), BF16),
            pltpu.VMEM((Z - 1, B, D), BF16),
            pltpu.VMEM((Z - 1, B, D), BF16),
            pltpu.VMEM((Q, F), F32),
            pltpu.VMEM((2, 2, YH, R, F), BF16),
            pltpu.VMEM((2, 2, YH, R, F), BF16),
            pltpu.VMEM((2, R, F), F32),
            pltpu.VMEM((R, F), BF16),
            pltpu.VMEM((R, F), BF16),
            dma((X + 2 * C + 1,)),
            dma((2, Z, S)),
            dma((2, Z, S)),
            dma((Z,)),
            dma((Z,)),
            dma((3,)),
            dma((3,)),
            dma((3,)),
            dma((3,)),
            dma((6,)),
            dma((6,)),
            dma((X,)),
            dma((X,)),
            dma((2, Z - 1)),
            dma((2, Z - 1)),
            dma((2, 2, YH)),
            dma((2, 2, YH)),
            dma,
            dma,
        ],
        compiler_params=pltpu.CompilerParams(
            collective_id=0, has_side_effects=True, vmem_limit_bytes=50 * 1024 * 1024
        ),
        cost_estimate=pl.CostEstimate(
            flops=6 * T * D * F, bytes_accessed=4 * D * F, transcendentals=T * F
        ),
    )(
        mantissas,
        exponents,
        weight.reshape(HY, X, R, F),
        cotangent.reshape(Z, C, B, F),
    )
    return out.reshape(T, F), dx, dw


def solution(mesh, sizes=SIZES):
    n = SimpleNamespace(**vars(sizes), S=4)
    return jax.shard_map(
        functools.partial(body, n),
        mesh=mesh,
        in_specs=(
            P(("dp", "tensor"), None),
            P(("dp", "tensor"), None),
            P(None, "tensor"),
            P("dp", "tensor"),
        ),
        out_specs=(P("dp", "tensor"), P(("dp", "tensor"), None), P("dp", "tensor")),
        check_vma=False,
    )
```

time: 1080 us -> 76.6 us (0.07)
  the two profiles are of different devices: /device:TPU:6 before, /device:TPU:8 now
where the time goes in v1:
time: 76.6 us; the launch traced here: 76.4 us
  Pallas kernels  71.3 us (93%)
  local copies, waits for them, and re-layouts  4.51 us (6%)
    pallas_call x1, Pallas kernels, body(): pl.pallas_call(functools.partial(kernel, n), out_shape=(jax.ShapeDtypeStr...  71.3 us
    unnamed x9, local copies, waits for them, and re-layouts  4.51 us

profile of v1, /device:TPU:8, one launch (start us, length us, event | category | flops | bytes accessed | tf_op | source)
XLA Modules:
  0.0 76.4 jit_solution(11545046353831328676)
XLA Ops:
  0.6 0.0 copy-start
  0.6 0.9 %copy-done = bf16[192,640]{1,0:T(8,128)(2,1)S(1)} copy-done((bf16[192,640]{1,0:T(8,128)(2,1)S(1)}, bf16[192,640]{1,0:T(8,128)(2,1)}, u32[]{:S(2)}) %copy-start) | copy-done | bytes 245784
  1.6 0.0 copy-start.1
  1.6 0.9 %copy-done.1 = bf16[16,3072]{1,0:T(8,128)(2,1)S(1)} copy-done((bf16[16,3072]{1,0:T(8,128)(2,1)S(1)}, bf16[16,3072]{1,0:T(8,128)(2,1)}, u32[]{:S(2)}) %copy-start.1) | copy-done | bytes 98328
  2.5 0.0 copy-start.2
  2.5 0.7 copy-done.2
  3.2 71.3 %shard_map.67 = (bf16[6,2,16,640]{3,2,1,0:T(8,128)(2,1)S(1)}, bf16[16,3072]{1,0:T(8,128)(2,1)S(1)}, f32[48,640]{1,0:T(8,128)S(1)}) custom-call(bf16[16,3072]{1,0:T(8,128)(2,1)S(1)} %copy-done.1, s32[16,24]{1,0:T(8,128)S(1)} %copy-done.2, bf16[16,4,48,640]{3,2,1,0:T(8,128)(2,1)} %bitcast.5, bf16[6,2,16,640]{3,2,1,0:T(8,128)(2,1)S(1)} %bitcast.4), custom_call_target="tpu_custom_call" | custom-call | flops 2264924160 | bytes 7864320 | tf_op jit(solution)/shard_map/pallas_call | solution.py:425
  74.4 0.7 copy.10
  75.1 0.6 copy.11
  75.8 0.6 copy.12
Async XLA Ops:
  0.6 0.9 %copy-start = (bf16[192,640]{1,0:T(8,128)(2,1)S(1)}, bf16[192,640]{1,0:T(8,128)(2,1)}, u32[]{:S(2)}) copy-start(bf16[192,640]{1,0:T(8,128)(2,1)} %param.7) | copy-start | bytes 737284
  1.6 0.9 %copy-start.1 = (bf16[16,3072]{1,0:T(8,128)(2,1)S(1)}, bf16[16,3072]{1,0:T(8,128)(2,1)}, u32[]{:S(2)}) copy-start(bf16[16,3072]{1,0:T(8,128)(2,1)} %mant.1) | copy-start | bytes 294916
  2.5 0.7 copy-start.2

commit v2 on v0

v2 whole, which is shorter than its diff:
```python
import functools
import math
from types import SimpleNamespace

import jax
import jax.numpy as jnp
from jax import lax
from jax.experimental import pallas as pl
from jax.experimental.pallas import tpu as pltpu
from jax.sharding import PartitionSpec as P

MESH = pl.DeviceIdType.MESH
F32, BF16 = jnp.float32, jnp.bfloat16

SIZES = SimpleNamespace(H=2, Y=8, X=4, Z=6, C=2, B=16, R=48, F=640)
GROUP = 2


def permute_tiles(tiles, size, out_chunk_source):
    lane = lax.broadcasted_iota(jnp.int32, tiles[0].shape, 1)
    result = []
    for k in range(len(tiles)):
        runs = []
        for l in range(128):
            o = k * 128 + l
            src = out_chunk_source(o // size) * size + o % size
            key = (src // 128, (l - src) % 128)
            if runs and runs[-1][0] == key:
                runs[-1][2] = l + 1
            else:
                runs.append([key, l, l + 1])
        out = None
        for (tile, shift), lo, hi in runs:
            piece = tiles[tile]
            if shift:
                piece = pltpu.roll(piece, shift, 1)
            out = piece if out is None else jnp.where(lane >= lo, piece, out)
        result.append(out)
    return result


def kernel(
    n,
    mant_hbm, expo_hbm, w_hbm, ct_hbm,
    out_hbm, dx_out, dw_out,
    mant, expo, wp, wn, ct, xg, xq, gq, outv, prt, psib, dx_in, dx_send, dx_sum, acc, ysend, yrecv, tu, hsend, hrecv,
    loc, ag_s, ag_r, sib_s, sib_r, xs_s, xs_r, xb_s, xb_r, g_s, g_r, p_s, p_r, dx_s, dx_r, y_s, y_r,
    h_s, h_r, h_ready,
):
    H, Y, X, Z, C, B, R, F = n.H, n.Y, n.X, n.Z, n.C, n.B, n.R, n.F
    HY = H * Y
    D = HY * X * R
    Q = D // X
    NB = Z // GROUP
    BC = GROUP * B
    BT = C * BC
    T = NB * BT
    S = n.S
    SB = D // S
    FA = (F // 128 + 1) // 2 * 128

    dp = lax.axis_index("dp")
    tp = lax.axis_index("tensor")
    x = lax.rem(dp, X)
    y = lax.rem(dp // X, Y)
    h = dp // (X * Y)
    c = lax.rem(tp, C)
    z = tp // C
    plane = dp - x

    sib = (dp, tp + 1 - 2 * c)
    z_by = {(0, 1): (dp, tp + C), (0, 2): (dp, tp + 2 * C), (1, 1): (dp, tp - C), (1, 2): (dp, tp - 2 * C)}
    x_by = {k: (plane + lax.rem(x + k, X), tp) for k in (1, 2, 3)}
    y_by = {
        (way, k): ((h * Y + lax.rem(y + (k if way == 0 else Y - k), Y)) * X + x, tp) for way in (0, 1) for k in (1, 2)
    }
    h_by = (((1 - h) * Y + y) * X + x, tp)

    behind = (z, Z - 1 - z)
    ahead = (Z - 1 - z, z)

    def remote(src, dst, send, recv, device):
        return pltpu.make_async_remote_copy(
            src_ref=src, dst_ref=dst, send_sem=send, recv_sem=recv,
            device_id=device, device_id_type=MESH,
        )

    def arrived(dst, recv):
        remote(dst, dst, recv, recv, sib).wait_recv()

    def sent(src, send):
        remote(src, src, send, send, sib).wait_send()

    mant_in = pltpu.make_async_copy(mant_hbm, mant, loc.at[0])
    expo_in = pltpu.make_async_copy(expo_hbm, expo, loc.at[1])
    w_in = [pltpu.make_async_copy(w_hbm.at[:, k], wp.at[k], loc.at[2 + k]) for k in range(X)]
    ct_in = [pltpu.make_async_copy(ct_hbm.at[:, :, k], ct.at[:, k], loc.at[2 + X + k]) for k in range(C)]
    wn_in = pltpu.make_async_copy(w_hbm, wn, loc.at[2 + X + C])
    for copy in [mant_in, expo_in, *w_in, *ct_in, wn_in]:
        copy.start()

    barrier = pltpu.get_barrier_semaphore()

    def greet(device):
        pl.semaphore_signal(barrier, inc=1, device_id=device, device_id_type=MESH)

    for device in [sib, x_by[1], x_by[2], x_by[3], *y_by.values()]:
        greet(device)

    for way in (0, 1):
        for k in (1, 2):
            @pl.when(ahead[way] >= k)
            def _():
                greet(z_by[way, k])

    @pl.when(h == 0)
    def _():
        greet(h_by)

    def row(core, q):
        return (q // GROUP) * BT + core * BC + lax.rem(q, GROUP) * B

    def rows(core, q):
        return pl.ds(pl.multiple_of(row(core, q), B), B)

    def part_rows(core, b):
        return pl.ds(pl.multiple_of(b * BT + core * BC, BC), BC)

    mant_in.wait()
    expo_in.wait()
    factors = jnp.exp2(expo[...].astype(F32))
    tiles = [
        mant[:, pl.ds(128 * b, 128)].astype(F32) * factors[:, b : b + 1]
        for b in range(D // 128)
    ]
    for k, tile in enumerate(permute_tiles(tiles, R, lambda j: (j % HY) * X + j // HY)):
        xg[rows(c, z), pl.ds(128 * k, 128)] = tile.astype(BF16)

    count = 8 + h
    for way in (0, 1):
        count = count + jnp.minimum(ahead[way], 2)
    pl.semaphore_wait(barrier, count)

    @pl.when(h == 1)
    def _():
        pl.semaphore_signal(h_ready, inc=1, device_id=h_by, device_id_type=MESH)

    def block(way, far):
        return z - far if way == 0 else z + far

    def hop(way, far, k, sub):
        part = xg.at[rows(c, block(way, far)), pl.ds(sub * SB, SB)]
        at = far + k - 1
        return remote(part, part, ag_s.at[way, at, sub], ag_r.at[way, at, sub], z_by[way, k])

    def gathered(way, far, sub):
        arrived(xg.at[rows(c, block(way, far)), pl.ds(sub * SB, SB)], ag_r.at[way, far - 1, sub])

    def hops(far, act, sub, ways=(0, 1)):
        for way in ways:
            for k in (2, 1):
                if far + k < Z:
                    @pl.when((behind[way] >= far) & (ahead[way] >= k))
                    def _():
                        act(hop(way, far, k, sub))

    def spread_sibling(q):
        part = xg.at[rows(c, q), :]
        return remote(part, part, sib_s.at[q], sib_r.at[q], sib)

    def spread_x(q, k):
        to = lax.rem(x + k, X)
        at = pl.ds(pl.multiple_of(c * BC + lax.rem(q, GROUP) * B, B), B)
        return remote(
            xg.at[rows(c, q), pl.ds(pl.multiple_of(to * Q, Q), Q)],
            xq.at[q // GROUP, k, at, :],
            xs_s.at[k], xs_r.at[k, q // GROUP], x_by[k],
        )

    def spread(q):
        spread_sibling(q).start()
        for k in (2, 1, 3):
            spread_x(q, k).start()

    for sub in range(S):
        hops(0, lambda copy: copy.start(), sub)
    spread(z)

    def gather_step(far):
        for sub in range(S):
            for way in (0, 1):
                @pl.when(behind[way] >= far)
                def _():
                    gathered(way, far, sub)
                    if far % 2 == 0:
                        for k in (2, 1):
                            if far + k < Z:
                                @pl.when(ahead[way] >= k)
                                def _():
                                    hop(way, far, k, sub).start()

        for way in (0, 1):
            @pl.when(behind[way] >= far)
            def _():
                spread(block(way, far))

    def drain_gather():
        for far in range(0, Z, 2):
            for sub in range(S):
                hops(far, lambda copy: copy.wait_send(), sub)
        for q in range(Z):
            spread_sibling(q).wait_send()
        for k in (1, 2, 3):
            sent(xq.at[:, k, pl.ds(0, BC), :], xs_s.at[k])

    def batch(i):
        return jnp.where(z < Z // 2, i, NB - 1 - i)

    def g_part(b, k):
        return remote(gq.at[b, 0], gq.at[b, k], g_s.at[b, k], g_r.at[b, k], x_by[k])

    def forward(b):
        for i in range(GROUP):
            q = b * GROUP + i
            arrived(xg.at[rows(1 - c, q), :], sib_r.at[q])
        tokens = pl.ds(pl.multiple_of(b * BT, BT), BT)
        linear = jnp.dot(xg[tokens, pl.ds(0, Q)], wp[0].reshape(Q, F), preferred_element_type=F32)
        for k in range(1, X):
            linear = linear + jnp.dot(
                xg[tokens, pl.ds(k * Q, Q)], wp[k].reshape(Q, F), preferred_element_type=F32
            )
        sigmoid = jax.nn.sigmoid(linear)
        cot = ct[b].reshape(BT, F).astype(F32)
        gq[b, 0] = (cot * sigmoid * (1.0 + linear * (1.0 - sigmoid))).astype(BF16)
        for k in (2, 1, 3):
            g_part(b, k).start()
        outv[b] = (linear * sigmoid).astype(BF16).reshape(C, GROUP, B, F)
        xq[b, 0] = xg[tokens, pl.ds(pl.multiple_of(x * Q, Q), Q)]

    def x_sibling(b, k):
        part = xq.at[b, k, pl.ds(pl.multiple_of(c * BC, BC), BC), :]
        return remote(part, part, xb_s.at[b, k], xb_r.at[b, k], sib)

    def x_pass(b):
        for k in (1, 3, 2):
            arrived(xq.at[b, k, pl.ds(0, BC), :], xs_r.at[k, b])
            x_sibling(b, k).start()

    def dw_batch(b, first):
        for k in (1, 3, 2):
            x_sibling(b, k).wait_recv()
            g_part(b, k).wait_recv()
        part = lax.dot_general(
            xq[b].reshape(4 * BT, Q), gq[b].reshape(4 * BT, F),
            (((0,), (0,)), ((), ())), preferred_element_type=F32,
        )
        if first:
            acc[...] = part
        else:
            acc[...] += part

    order = [far for pair_of in ((2, 1), (4, 3), (6, 5)) for far in pair_of if far < Z]
    for copy in [*w_in, *ct_in]:
        copy.wait()
    for i in range(NB):
        for far in order[2 * i : 2 * i + 2] if i < NB - 1 else order[2 * i :]:
            gather_step(far)
        forward(batch(i))
        if i < NB - 1:
            x_pass(batch(i))

    out_back = [
        pltpu.make_async_copy(outv.at[:, k], out_hbm.at[:, :, k], loc.at[3 + X + C + k]) for k in range(C)
    ]
    for copy in out_back:
        copy.start()


    wn_in.wait()
    NC = X
    ND = D // NC

    def p_sibling(b, k):
        columns = pl.ds(k * ND, ND)
        return remote(
            prt.at[part_rows(1 - c, b), columns],
            psib.at[pl.ds(b * BC, BC), columns],
            p_s.at[b, k], p_r.at[b, k], sib,
        )

    grads = gq[:, 0].reshape(T, F)
    for k in range(NC):
        part = lax.dot_general(
            grads, wn[pl.ds(k * (HY // NC), HY // NC)].reshape(ND, F),
            (((1,), (1,)), ((), ())), preferred_element_type=F32,
        )
        prt[:, pl.ds(k * ND, ND)] = part.astype(BF16)
        for b in range(NB):
            p_sibling(b, k).start()

    def drain_g():
        for copy in out_back:
            copy.wait()
        for b in range(NB):
            for k in (1, 2, 3):
                x_sibling(b, k).wait_send()
                g_part(b, k).wait_send()
            for k in range(NC):
                p_sibling(b, k).wait_send()

    def pair(q):
        own = prt[rows(c, q), :].astype(F32)
        return own + psib[pl.ds(pl.multiple_of(q * B, B), B), :].astype(F32)

    def dx_to(way, far):
        return z + far if way == 0 else z - far

    def dx_hop(way, q, k):
        return remote(
            dx_send.at[way, q], dx_in.at[way, k - 1, q], dx_s.at[way, q], dx_r.at[way, k - 1, q], z_by[way, k]
        )

    def dx_add(way, q):
        for k in (1, 2):
            @pl.when(behind[way] >= k)
            def _():
                arrived(dx_in.at[way, k - 1, q], dx_r.at[way, k - 1, q])
                dx_sum[...] += dx_in[way, k - 1, q].astype(F32)

    def dx_step(far):
        if far >= Z:
            return
        for way in (0, 1):
            @pl.when(ahead[way] >= far)
            def _():
                q = dx_to(way, far)
                if far % 2 == 1:
                    dx_send[way, q] = pair(q).astype(BF16)
                else:
                    dx_sum[...] = pair(q)
                    dx_add(way, q)
                    dx_send[way, q] = dx_sum[...].astype(BF16)
                dx_hop(way, q, 2 - far % 2).start()

    def drain_dx():
        for far in range(1, Z):
            for way in (0, 1):
                @pl.when(ahead[way] >= far)
                def _():
                    dx_hop(way, dx_to(way, far), 2 - far % 2).wait_send()

    x_pass(batch(NB - 1))
    for i in range(NB - 1):
        dw_batch(batch(i), i == 0)
    for b in range(NB):
        for k in range(NC):
            p_sibling(b, k).wait_recv()
    for far in (5, 3, 1):
        dx_step(far)

    unit = [1 - h, h]
    share = (pl.ds(0, FA), pl.ds(FA, F - FA))

    def y_rows(i, to):
        return pl.ds(pl.multiple_of((unit[i] * Y + to) * R, R), R)

    def y_own(way, i, far):
        return acc[y_rows(i, lax.rem(y + (far if way == 0 else Y - far), Y)), :]

    def y_hop(way, i, part):
        src, dst = ysend.at[way, i, part], yrecv.at[way, i, part]
        if part == 1:
            src, dst = src.at[:, share[way]], dst.at[:, share[way]]
        return remote(src, dst, y_s.at[way, i, part], y_r.at[way, i, part], y_by[way, 1 + part % 2])

    def y_start(way, i, part):
        ysend[way, i, part] = y_own(way, i, (3, 4, 1)[part]).astype(BF16)
        y_hop(way, i, part).start()

    def y_relay(way, i):
        y_hop(way, i, 0).wait_recv()
        y_hop(way, i, 1).wait_recv()
        far = yrecv[way, i, 1, :, share[way]].astype(F32)
        none = jnp.zeros((R, F - far.shape[1]), F32)
        far = jnp.concatenate([far, none] if way == 0 else [none, far], axis=1)
        value = y_own(way, i, 2) + yrecv[way, i, 0].astype(F32) + far
        ysend[way, i, 3] = value.astype(BF16)
        y_hop(way, i, 3).start()

    def y_total(i):
        value = acc[y_rows(i, y), :]
        for part in (2, 3):
            for way in (0, 1):
                y_hop(way, i, part).wait_recv()
                value = value + yrecv[way, i, part].astype(F32)
        return value

    def drain_y():
        for way in (0, 1):
            for i in (0, 1):
                for part in range(4):
                    y_hop(way, i, part).wait_send()

    dw_batch(batch(NB - 1), NB == 1)


    for i in (0, 1):
        for part in (0, 1):
            for way in (0, 1):
                y_start(way, i, part)
    for i in (0, 1):
        for way in (0, 1):
            y_start(way, i, 2)
    dx_step(4)
    for i in (0, 1):
        for way in (0, 1):
            y_relay(way, i)
    dx_step(2)

    hsend[...] = y_total(0).astype(BF16)

    @pl.when(h == 0)
    def _():
        pl.semaphore_wait(h_ready, 1)

    across = remote(hsend, hrecv, h_s, h_r, h_by)
    across.start()
    tu[...] = y_total(1)

    dx_sum[...] = pair(z)
    for way in (0, 1):
        dx_add(way, z)
    dx_out[...] = dx_sum[...].astype(BF16)

    drain_gather()
    drain_g()
    drain_dx()
    drain_y()

    across.wait_recv()
    factor = 1.0 / math.sqrt(H * Y * X * T)
    dw_out[...] = (tu[...] + hrecv[...].astype(F32)) * factor
    across.wait_send()


def body(n, mantissas, exponents, weight, cotangent):
    H, Y, X, Z, C, B, R, F = n.H, n.Y, n.X, n.Z, n.C, n.B, n.R, n.F
    HY = H * Y
    D = HY * X * R
    Q, T, S = D // X, Z * B * C, n.S
    NB, BC = Z // GROUP, GROUP * B
    BT = C * BC
    anywhere = pl.BlockSpec(memory_space=pl.ANY)
    hbm = pl.BlockSpec(memory_space=pltpu.HBM)
    vmem = pl.BlockSpec(memory_space=pltpu.VMEM)
    dma = pltpu.SemaphoreType.DMA
    out, dx, dw = pl.pallas_call(
        functools.partial(kernel, n),
        out_shape=(
            jax.ShapeDtypeStruct((NB, GROUP, C, B, F), BF16),
            jax.ShapeDtypeStruct((B, D), BF16),
            jax.ShapeDtypeStruct((R, F), F32),
        ),
        in_specs=[hbm] * 4,
        out_specs=(anywhere, vmem, vmem),
        scratch_shapes=[
            pltpu.VMEM((B, D), BF16),
            pltpu.VMEM((B, D // 128), jnp.int32),
            pltpu.VMEM((X, HY, R, F), BF16),
            pltpu.VMEM((HY, X, R, F), BF16),
            pltpu.VMEM((NB, C, GROUP, B, F), BF16),
            pltpu.VMEM((T, D), BF16),
            pltpu.VMEM((NB, 4, BT, Q), BF16),
            pltpu.VMEM((NB, 4, BT, F), BF16),
            pltpu.VMEM((NB, C, GROUP, B, F), BF16),
            pltpu.VMEM((T, D), BF16),
            pltpu.VMEM((Z * B, D), BF16),
            pltpu.VMEM((2, 2, Z, B, D), BF16),
            pltpu.VMEM((2, Z, B, D), BF16),
            pltpu.VMEM((B, D), F32),
            pltpu.VMEM((Q, F), F32),
            pltpu.VMEM((2, 2, 4, R, F), BF16),
            pltpu.VMEM((2, 2, 4, R, F), BF16),
            pltpu.VMEM((R, F), F32),
            pltpu.VMEM((R, F), BF16),
            pltpu.VMEM((R, F), BF16),
            dma((3 + X + 2 * C,)),
            dma((2, Z, S)),
            dma((2, Z, S)),
            dma((Z,)),
            dma((Z,)),
            dma((4,)),
            dma((4, NB)),
            dma((NB, 4)),
            dma((NB, 4)),
            dma((NB, 4)),
            dma((NB, 4)),
            dma((NB, X)),
            dma((NB, X)),
            dma((2, Z)),
            dma((2, 2, Z)),
            dma((2, 2, 4)),
            dma((2, 2, 4)),
            dma,
            dma,
            pltpu.SemaphoreType.REGULAR,
        ],
        compiler_params=pltpu.CompilerParams(
            collective_id=0, has_side_effects=True, vmem_limit_bytes=62 * 1024 * 1024
        ),
        cost_estimate=pl.CostEstimate(
            flops=6 * T * D * F, bytes_accessed=4 * D * F, transcendentals=T * F
        ),
    )(
        mantissas,
        exponents,
        weight.reshape(HY, X, R, F),
        cotangent.reshape(NB, GROUP, C, B, F),
    )
    return out.reshape(T, F), dx, dw


def solution(mesh, sizes=SIZES):
    n = SimpleNamespace(**vars(sizes), S=2)
    return jax.shard_map(
        functools.partial(body, n),
        mesh=mesh,
        in_specs=(
            P(("dp", "tensor"), None),
            P(("dp", "tensor"), None),
            P(None, "tensor"),
            P("dp", "tensor"),
        ),
        out_specs=(P("dp", "tensor"), P(("dp", "tensor"), None), P("dp", "tensor")),
        check_vma=False,
    )
```

time: 1080 us -> 73.8 us (0.07)
  waiting for transfers between devices: 1050 us -> 0 us
  Pallas kernels: 0 us -> 67.5 us
  matrix products: 13.6 us -> 0 us
  between operations: 13.8 us -> 0.64 us
    reduce_scatter x2 -> x0, waiting for transfers between devices: 976 us -> none  [the longest x1 907 us: body(): lax.psum_scatter(lax.dot_general(gathered, grad_linear, (((0,), (0,)), ((...]
    all_gather x1 -> x0, waiting for transfers between devices: 75.7 us -> none  [body(): gathered = lax.all_gather(local_rows, 'tensor', axis=0, tiled=True)]
    pallas_call x0 -> x1, Pallas kernels: none -> 67.5 us  [body(): pl.pallas_call(functools.partial(kernel, n), out_shape=(jax.ShapeDtypeStr...]
    dot_general x3 -> x0, matrix products: 13.6 us -> none  [the longest x1 4.71 us: body(): lax.dot_general(grad_linear, weight, (((1,), (1,)), ((), ())), preferred_...]
  transfers between devices with their start and end apart: 3 -> 0, of which waited for: 3 -> 0; matrix products, arithmetic and copies ran while one was open for 1% -> 0% of each run, Pallas kernels for 0% -> 0%
where the time goes in v2:
time: 73.8 us; the launch traced here: 72.9 us
  Pallas kernels  67.5 us (91%)
  local copies, waits for them, and re-layouts  4.75 us (6%)
    pallas_call x1, Pallas kernels, body(): pl.pallas_call(functools.partial(kernel, n), out_shape=(jax.ShapeDtypeStr...  67.5 us
    unnamed x3, local copies, waits for them, and re-layouts  4.75 us

profile of v2, /device:TPU:6, one launch (start us, length us, event | category | flops | bytes accessed | tf_op | source)
XLA Modules:
  0.0 72.9 jit_solution(12560916604705474347)
XLA Ops:
  0.6 67.5 %shard_map.67 = (bf16[3,2,2,16,640]{4,3,2,1,0:T(8,128)(2,1)}, bf16[16,3072]{1,0:T(8,128)(2,1)}, f32[48,640]{1,0:T(8,128)}) custom-call(bf16[16,3072]{1,0:T(8,128)(2,1)} %mant_hbm.1, s32[16,24]{1,0:T(8,128)} %expo_hbm.1, bf16[16,4,48,640]{3,2,1,0:T(8,128)(2,1)} %bitcast.4, bf16[3,2,2,16,640]{4,3,2,1,0:T(8,128)(2,1)} %bitcast.5), custom_call_target="tpu_custom_call" | custom-call | flops 2264924160 | bytes 7864320 | tf_op jit(solution)/shard_map/pallas_call | solution.py:457
  68.1 1.7 %copy.10 = bf16[192,640]{1,0:T(8,128)(2,1)} copy(bf16[192,640]{1,0:T(8,128)(2,1)} %bitcast.3) | data formatting | bytes 491520
  69.8 1.5 %copy.11 = bf16[16,3072]{1,0:T(8,128)(2,1)} copy(bf16[16,3072]{1,0:T(8,128)(2,1)} %get-tuple-element.13) | data formatting | bytes 196608
  71.3 1.6 %copy.12 = f32[48,640]{1,0:T(8,128)} copy(f32[48,640]{1,0:T(8,128)} %get-tuple-element.14) | data formatting | bytes 245760

commit v3 on v2

--- a/solution.py
+++ b/solution.py
@@ -506,16 +506,21 @@
             pltpu.SemaphoreType.REGULAR,
         ],
         compiler_params=pltpu.CompilerParams(
-            collective_id=0, has_side_effects=True, vmem_limit_bytes=62 * 1024 * 1024
+            collective_id=0, has_side_effects=True, vmem_limit_bytes=50 * 1024 * 1024
         ),
         cost_estimate=pl.CostEstimate(
             flops=6 * T * D * F, bytes_accessed=4 * D * F, transcendentals=T * F
         ),
     )(
-        mantissas,
-        exponents,
-        weight.reshape(HY, X, R, F),
-        cotangent.reshape(NB, GROUP, C, B, F),
+        *(
+            pltpu.with_memory_space_constraint(a, pltpu.HBM)
+            for a in (
+                mantissas,
+                exponents,
+                weight.reshape(HY, X, R, F),
+                cotangent.reshape(NB, GROUP, C, B, F),
+            )
+        ),
     )
     return out.reshape(T, F), dx, dw
 

time: 73.8 us -> 70.3 us (0.953)
  local copies, waits for them, and re-layouts: 4.75 us -> 1.98 us
    unnamed x3, local copies, waits for them, and re-layouts: 4.75 us -> 1.98 us
where the time goes in v3:
time: 70.3 us; the launch traced here: 69.4 us
  Pallas kernels  66.8 us (95%)
  local copies, waits for them, and re-layouts  1.98 us (3%)
    pallas_call x1, Pallas kernels, body(): pl.pallas_call(functools.partial(kernel, n), out_shape=(jax.ShapeDtypeStr...  66.8 us
    unnamed x3, local copies, waits for them, and re-layouts  1.98 us

profile of v3, /device:TPU:6, one launch (start us, length us, event | category | flops | bytes accessed | tf_op | source)
XLA Modules:
  0.0 69.4 jit_solution(5508768510126849629)
XLA Ops:
  0.6 66.8 %shard_map.67 = (bf16[3,2,2,16,640]{4,3,2,1,0:T(8,128)(2,1)S(1)}, bf16[16,3072]{1,0:T(8,128)(2,1)S(1)}, f32[48,640]{1,0:T(8,128)S(1)}) custom-call(bf16[16,3072]{1,0:T(8,128)(2,1)} %mant_hbm.1, s32[16,24]{1,0:T(8,128)} %expo_hbm.1, bf16[16,4,48,640]{3,2,1,0:T(8,128)(2,1)} %bitcast.4, bf16[3,2,2,16,640]{4,3,2,1,0:T(8,128)(2,1)} %bitcast.5), custom_call_target="tpu_custom_call" | custom-call | flops 2264924160 | bytes 7864320 | tf_op jit(solution)/shard_map/pallas_call | solution.py:457
  67.4 0.7 %copy.10 = bf16[192,640]{1,0:T(8,128)(2,1)} copy(bf16[192,640]{1,0:T(8,128)(2,1)S(1)} %bitcast.3) | data formatting | bytes 491520
  68.1 0.6 copy.11
  68.8 0.6 copy.12

commit v4 on v3

--- a/solution.py
+++ b/solution.py
@@ -404,18 +404,15 @@
     dw_batch(batch(NB - 1), NB == 1)
 
 
-    for i in (0, 1):
-        for part in (0, 1):
-            for way in (0, 1):
-                y_start(way, i, part)
-    for i in (0, 1):
+    for part in range(3):
         for way in (0, 1):
-            y_start(way, i, 2)
+            y_start(way, 0, part)
+    for way in (0, 1):
+        y_relay(way, 0)
+    for part in range(3):
+        for way in (0, 1):
+            y_start(way, 1, part)
     dx_step(4)
-    for i in (0, 1):
-        for way in (0, 1):
-            y_relay(way, i)
-    dx_step(2)
 
     hsend[...] = y_total(0).astype(BF16)
 
@@ -425,6 +422,9 @@
 
     across = remote(hsend, hrecv, h_s, h_r, h_by)
     across.start()
+    for way in (0, 1):
+        y_relay(way, 1)
+    dx_step(2)
     tu[...] = y_total(1)
 
     dx_sum[...] = pair(z)

time: 70.3 us -> 67.3 us (0.957)
  Pallas kernels: 66.8 us -> 63.7 us
    pallas_call x1, Pallas kernels: 66.8 us -> 63.7 us  [body(): pl.pallas_call(functools.partial(kernel, n), out_shape=(jax.ShapeDtypeStr...]
where the time goes in v4:
time: 67.3 us; the launch traced here: 66.4 us
  Pallas kernels  63.7 us (95%)
  local copies, waits for them, and re-layouts  1.98 us (3%)
    pallas_call x1, Pallas kernels, body(): pl.pallas_call(functools.partial(kernel, n), out_shape=(jax.ShapeDtypeStr...  63.7 us
    unnamed x3, local copies, waits for them, and re-layouts  1.98 us

profile of v4, /device:TPU:6, one launch (start us, length us, event | category | flops | bytes accessed | tf_op | source)
XLA Modules:
  0.0 66.4 jit_solution(17533207605617476875)
XLA Ops:
  0.6 63.7 %shard_map.67 = (bf16[3,2,2,16,640]{4,3,2,1,0:T(8,128)(2,1)S(1)}, bf16[16,3072]{1,0:T(8,128)(2,1)S(1)}, f32[48,640]{1,0:T(8,128)S(1)}) custom-call(bf16[16,3072]{1,0:T(8,128)(2,1)} %mant_hbm.1, s32[16,24]{1,0:T(8,128)} %expo_hbm.1, bf16[16,4,48,640]{3,2,1,0:T(8,128)(2,1)} %bitcast.4, bf16[3,2,2,16,640]{4,3,2,1,0:T(8,128)(2,1)} %bitcast.5), custom_call_target="tpu_custom_call" | custom-call | flops 2264924160 | bytes 7864320 | tf_op jit(solution)/shard_map/pallas_call | solution.py:457
  64.4 0.7 %copy.10 = bf16[192,640]{1,0:T(8,128)(2,1)} copy(bf16[192,640]{1,0:T(8,128)(2,1)S(1)} %bitcast.3) | data formatting | bytes 491520
  65.1 0.6 copy.11
  65.7 0.6 copy.12
